TPU v7x, 32 devices: a whole 2x2x4 slice. The times are simulated.
32 devices in a mesh: groups: 2 (over x), owner: 8 (over z, y), tile: 2 (over core).
Axes of the slice: x: 2, y: 2, z: 4, core: 2. Of those that a mesh axis runs over, the one named last changes fastest.
Arguments:
- embeddings: bfloat16 [32768, 768], P(('groups', 'owner', 'tile')), parts along dimension 0, may hold values from -8 to 8
- cluster_ids: int32 [32768], P(('groups', 'owner', 'tile')), parts along dimension 0, may hold values from 0 to 15, as said below
Outputs:
- dup_score: float32 [32768], P(('groups', 'owner', 'tile')), parts along dimension 0
There are 2 independent parts, one for each index of `groups`. A program takes and returns all parts, laid end to end along the dimension named above; each array names one. Nothing has to cross between parts.
Inputs may be any that keep to these rules, and one draw needn't show every extreme that they name: `cluster_ids`: in each aligned block of 1024 rows (the rows of one device) no cluster is named more than 128 times; some cluster is named exactly 128 times in every block.
All inputs are finite; a program needn't handle non-finite values.
Results may differ from a plain program's by a relative error of at most 0.0045.
Values may be sent and summed in bfloat16 or wider, within the bound.
A program may use at most 64 MiB of HBM per device.

v0:
```python
import jax
import jax.numpy as jnp
import numpy as np
from jax import lax
from jax.sharding import PartitionSpec as P

CLUS_OWN = 2


epsilon = 1e-06
sharpness = 20.0


def unit_rows(embeddings):
    values = embeddings.astype(jnp.float32)
    scale = lax.rsqrt(jnp.sum(values * values, axis=1, keepdims=True) + epsilon)
    return (values * scale).astype(jnp.bfloat16)


def pair_table(clusters_here, blocks_per):
    entries = [
        (cluster_index, first_block, second_block)
        for cluster_index in range(clusters_here)
        for first_block in range(blocks_per)
        for second_block in range(first_block, blocks_per)
    ]
    return np.array(entries, dtype=np.int32)


def kernel_sums(member_rows, member_flags, table):
    clusters_here, members, width = member_rows.shape
    block = min(512, members)

    def one_pair(step, totals):
        entry = table[step]
        cluster_index = entry[0]
        first = entry[1] * block
        second = entry[2] * block
        left = lax.dynamic_slice(member_rows, (cluster_index, first, 0), (1, block, width))[0]
        right = lax.dynamic_slice(member_rows, (cluster_index, second, 0), (1, block, width))[0]
        left_flag = lax.dynamic_slice(member_flags, (cluster_index, first), (1, block))[0]
        right_flag = lax.dynamic_slice(member_flags, (cluster_index, second), (1, block))[0]
        cosine = lax.dot_general(
            left, right, (((1,), (1,)), ((), ())), preferred_element_type=jnp.float32
        )
        kernel = jnp.exp(sharpness * (cosine - 1.0)) * left_flag[:, None] * right_flag[None, :]
        across = jnp.sum(kernel, axis=1)
        downward = jnp.sum(kernel, axis=0) * (first != second).astype(jnp.float32)
        current = lax.dynamic_slice(totals, (cluster_index, first), (1, block))
        totals = lax.dynamic_update_slice(totals, current + across[None, :], (cluster_index, first))
        current = lax.dynamic_slice(totals, (cluster_index, second), (1, block))
        totals = lax.dynamic_update_slice(
            totals, current + downward[None, :], (cluster_index, second)
        )
        return totals

    start = jnp.zeros((clusters_here, members), jnp.float32)
    return lax.fori_loop(0, table.shape[0], one_pair, start)


def shards(embeddings, cluster_ids):
    owners = lax.axis_size("owner")
    tiles = lax.axis_size("tile")
    count_rows, width = embeddings.shape
    clusters = CLUS_OWN * owners
    capacity = 2 * count_rows // clusters
    members = owners * tiles * capacity
    blocks_per = members // min(512, members)
    unit = unit_rows(embeddings)
    onehot = (cluster_ids[:, None] == jnp.arange(clusters, dtype=jnp.int32)[None, :]).astype(
        jnp.int32
    )
    ranks = jnp.cumsum(onehot, axis=0) - 1
    within = jnp.sum(onehot * ranks, axis=1)
    target = cluster_ids * capacity + within
    outgoing = jnp.zeros((clusters * capacity, width), jnp.bfloat16).at[target].set(unit)
    flags = (
        jnp.zeros((clusters * capacity,), jnp.bfloat16)
        .at[target]
        .set(jnp.ones((count_rows,), jnp.bfloat16))
    )
    arrived = (
        lax.all_to_all(
            outgoing.reshape(CLUS_OWN, owners, capacity, width),
            "owner",
            split_axis=1,
            concat_axis=1,
            tiled=True,
        ),
        lax.all_to_all(
            flags.reshape(CLUS_OWN, owners, capacity),
            "owner",
            split_axis=1,
            concat_axis=1,
            tiled=True,
        ),
    )
    joined = (
        lax.all_gather(arrived[0], "tile", axis=1, tiled=True),
        lax.all_gather(arrived[1], "tile", axis=1, tiled=True),
    )
    member_rows = joined[0].reshape(CLUS_OWN, members, width)
    member_flags = joined[1].reshape(CLUS_OWN, members).astype(jnp.float32)
    table = jnp.asarray(pair_table(CLUS_OWN, blocks_per).reshape(-1, tiles, 3))
    mine = lax.dynamic_index_in_dim(table, lax.axis_index("tile"), 1, keepdims=False)
    totals = kernel_sums(member_rows, member_flags, mine)
    shares = lax.psum_scatter(
        totals.reshape(CLUS_OWN, tiles, owners * capacity), "tile", scatter_dimension=1, tiled=True
    )
    returned = lax.all_to_all(
        shares.reshape(CLUS_OWN, owners, capacity), "owner", split_axis=1, concat_axis=1, tiled=True
    )
    score = returned.reshape(-1)[target]
    return jnp.log(score)


def solution(mesh):
    placed = (P(("groups", "owner", "tile"), None), P(("groups", "owner", "tile")))
    return jax.shard_map(
        shards,
        mesh=mesh,
        in_specs=placed,
        out_specs=P(("groups", "owner", "tile")),
        check_vma=False,
    )
```

profile of v0, /device:TPU:0, one launch (start us, length us, event | category | flops | bytes accessed | tf_op | source)
XLA Modules:
  0.0 215.7 jit_solution(7074859678640862034)
XLA Ops:
  6.5 0.7 fusion.17
  7.2 4.5 %reduce-window.6 = s32[16,8,128]{2,1,0:T(8,128)S(1)} reduce-window(s32[16,8,128]{2,1,0:T(8,128)S(1)} %fusion.17, s32[]{:T(128)} %constant.113.clone.1), window={size=1x1x128 pad=0_0x0_0x127_0}, to_apply=%region_0.0 | reduce-window | flops 2080768 | bytes 131076 | tf_op jit(solution)/shard_map/reduce-window
  12.1 0.7 fusion.16
  12.9 0.7 broadcast_clamp_fusion
  13.6 1.8 fusion.9
  15.4 7.2 %scatter_custom_fusion = bf16[2048,768]{1,0:T(8,128)(2,1)S(1)} fusion(s32[1024]{0:T(1024)S(1)} %get-tuple-element.151, bf16[1024,768]{1,0:T(8,128)(2,1)} %param.5, f32[1024]{0:T(1024)S(1)} %add_rsqrt_fusion, bf16[]{:T(256)} %constant.117.clone.1), kind=kCustom, calls=%fused_computation.21 | custom fusion | flops 2359296 | bytes 4722690 | tf_op jit(solution)/shard_map/scatter | solution.py:76
  22.5 0.3 copy.21
  22.8 77.8 %all_to_all.15 = bf16[2,8,128,768]{3,2,0,1:T(8,128)(2,1)S(1)} all-to-all(bf16[2,8,128,768]{3,2,0,1:T(8,128)(2,1)S(1)} %copy.21), channel_id=1, replica_groups=mesh['groups'=2,'owner'=8,'tile'=2] {'owner'}, dimensions={1} | all-to-all | bytes 6291456 | tf_op jit(solution)/shard_map/all_to_all | solution.py:83
  100.6 2.0 copy.22
  102.6 7.6 %scatter_custom_fusion.1 = bf16[2048]{0:T(1024)(128)(2,1)S(1)} fusion(s32[1024]{0:T(1024)S(1)} %get-tuple-element.151, bf16[1024]{0:T(1024)(128)(2,1)S(1)} %broadcast.73, bf16[]{:T(256)} %constant.117.clone.1), kind=kCustom, calls=%fused_computation.37 | custom fusion | bytes 4098 | tf_op jit(solution)/shard_map/scatter | solution.py:80
  110.2 0.6 copy.23
  110.8 3.6 %all-to-all-start.1 = ((bf16[2,8,128]{2,0,1:T(2,128)(2,1)}), bf16[2,8,128]{2,0,1:T(2,128)(2,1)S(1)}, u32[]{:S(2)}, u32[]{:S(2)}) async-start(bf16[2,8,128]{2,0,1:T(2,128)(2,1)} %copy.23), calls=%async_computation.1 | async-start | bytes 8192 | tf_op jit(solution)/shard_map/all_to_all | solution.py:90
  114.5 0.6 dynamic-slice
  115.1 5.7 %all-to-all-done.1 = bf16[2,8,128]{2,0,1:T(2,128)(2,1)S(1)} async-done(((bf16[2,8,128]{2,0,1:T(2,128)(2,1)}), bf16[2,8,128]{2,0,1:T(2,128)(2,1)S(1)}, u32[]{:S(2)}, u32[]{:S(2)}) %all-to-all-start.1) | async-done | bytes 4128 | tf_op jit(solution)/shard_map/all_to_all | solution.py:90
  120.8 1.8 all_gather.7
  122.6 66.5 %while.15 = (s32[]{:T(128)}, f32[2,2048]{1,0:T(2,128)S(1)}, s32[10,3]{0,1:T(4,128)S(1)}, bf16[2,2048,768]{2,1,0:T(8,128)(2,1)}, f32[2,2048]{1,0:T(2,128)S(1)}, /...) while((s32[]{:T(128)}, f32[2,2048]{1,0:T(2,128)S(1)}, s32[10,3]{0,1:T(4,128)S(1)}, ...), condition=%wide.region_9.10_spmd, body=%wide.region_6.0_spmd.sunk | while | flops 404226560 | bytes 1616205 | solution.py:58
  122.7 0.6 fusion.26
  126.5 2.2 %fusion.28 = (f32[512]{0:T(512)S(1)}, f32[512]{0:T(512)S(1)}) fusion(f32[512]{0:T(512)S(1)} %bitcast.71, f32[512]{0:T(512)S(1)} %bitcast.70, bf16[2,2048,768]{2,1,0:T(8,128)(2,1)} %get-tuple-element.225, s32[]{:T(128)S(6)} %select_n.67, s32[]{:T(128)S(6)} %select_n.69, s32[]{:T(128)S(6)} %select_n.68), kind=kOutput, calls=%fused_computation.40.clone.1 | convolution fusion | flops 404225024 | bytes 1583104 | tf_op jit(solution)/shard_map/while/body/eval_jaxpr/dot_general | solution.py:43
  128.8 0.2 dynamic_update_slice.22
  129.1 0.2 dynamic_update_slice.23
  129.4 0.6 fusion.26
  133.2 2.2 %fusion.28 = (f32[512]{0:T(512)S(1)}, f32[512]{0:T(512)S(1)}) fusion(f32[512]{0:T(512)S(1)} %bitcast.71, f32[512]{0:T(512)S(1)} %bitcast.70, bf16[2,2048,768]{2,1,0:T(8,128)(2,1)} %get-tuple-element.225, s32[]{:T(128)S(6)} %select_n.67, s32[]{:T(128)S(6)} %select_n.69, s32[]{:T(128)S(6)} %select_n.68), kind=kOutput, calls=%fused_computation.40.clone.1 | convolution fusion | flops 404225024 | bytes 1583104 | tf_op jit(solution)/shard_map/while/body/eval_jaxpr/dot_general | solution.py:43
  135.4 0.2 dynamic_update_slice.22
  135.8 0.2 dynamic_update_slice.23
  136.1 0.6 fusion.26
  139.8 2.2 %fusion.28 = (f32[512]{0:T(512)S(1)}, f32[512]{0:T(512)S(1)}) fusion(f32[512]{0:T(512)S(1)} %bitcast.71, f32[512]{0:T(512)S(1)} %bitcast.70, bf16[2,2048,768]{2,1,0:T(8,128)(2,1)} %get-tuple-element.225, s32[]{:T(128)S(6)} %select_n.67, s32[]{:T(128)S(6)} %select_n.69, s32[]{:T(128)S(6)} %select_n.68), kind=kOutput, calls=%fused_computation.40.clone.1 | convolution fusion | flops 404225024 | bytes 1583104 | tf_op jit(solution)/shard_map/while/body/eval_jaxpr/dot_general | solution.py:43
  142.1 0.2 dynamic_update_slice.22
  142.7 0.6 fusion.26
  146.5 2.2 %fusion.28 = (f32[512]{0:T(512)S(1)}, f32[512]{0:T(512)S(1)}) fusion(f32[512]{0:T(512)S(1)} %bitcast.71, f32[512]{0:T(512)S(1)} %bitcast.70, bf16[2,2048,768]{2,1,0:T(8,128)(2,1)} %get-tuple-element.225, s32[]{:T(128)S(6)} %select_n.67, s32[]{:T(128)S(6)} %select_n.69, s32[]{:T(128)S(6)} %select_n.68), kind=kOutput, calls=%fused_computation.40.clone.1 | convolution fusion | flops 404225024 | bytes 1583104 | tf_op jit(solution)/shard_map/while/body/eval_jaxpr/dot_general | solution.py:43
  149.4 0.6 fusion.26
  153.1 2.2 %fusion.28 = (f32[512]{0:T(512)S(1)}, f32[512]{0:T(512)S(1)}) fusion(f32[512]{0:T(512)S(1)} %bitcast.71, f32[512]{0:T(512)S(1)} %bitcast.70, bf16[2,2048,768]{2,1,0:T(8,128)(2,1)} %get-tuple-element.225, s32[]{:T(128)S(6)} %select_n.67, s32[]{:T(128)S(6)} %select_n.69, s32[]{:T(128)S(6)} %select_n.68), kind=kOutput, calls=%fused_computation.40.clone.1 | convolution fusion | flops 404225024 | bytes 1583104 | tf_op jit(solution)/shard_map/while/body/eval_jaxpr/dot_general | solution.py:43
  156.0 0.6 fusion.26
  159.8 2.2 %fusion.28 = (f32[512]{0:T(512)S(1)}, f32[512]{0:T(512)S(1)}) fusion(f32[512]{0:T(512)S(1)} %bitcast.71, f32[512]{0:T(512)S(1)} %bitcast.70, bf16[2,2048,768]{2,1,0:T(8,128)(2,1)} %get-tuple-element.225, s32[]{:T(128)S(6)} %select_n.67, s32[]{:T(128)S(6)} %select_n.69, s32[]{:T(128)S(6)} %select_n.68), kind=kOutput, calls=%fused_computation.40.clone.1 | convolution fusion | flops 404225024 | bytes 1583104 | tf_op jit(solution)/shard_map/while/body/eval_jaxpr/dot_general | solution.py:43
  162.6 0.6 fusion.26
  166.4 2.2 %fusion.28 = (f32[512]{0:T(512)S(1)}, f32[512]{0:T(512)S(1)}) fusion(f32[512]{0:T(512)S(1)} %bitcast.71, f32[512]{0:T(512)S(1)} %bitcast.70, bf16[2,2048,768]{2,1,0:T(8,128)(2,1)} %get-tuple-element.225, s32[]{:T(128)S(6)} %select_n.67, s32[]{:T(128)S(6)} %select_n.69, s32[]{:T(128)S(6)} %select_n.68), kind=kOutput, calls=%fused_computation.40.clone.1 | convolution fusion | flops 404225024 | bytes 1583104 | tf_op jit(solution)/shard_map/while/body/eval_jaxpr/dot_general | solution.py:43
  169.3 0.6 fusion.26
  173.1 2.2 %fusion.28 = (f32[512]{0:T(512)S(1)}, f32[512]{0:T(512)S(1)}) fusion(f32[512]{0:T(512)S(1)} %bitcast.71, f32[512]{0:T(512)S(1)} %bitcast.70, bf16[2,2048,768]{2,1,0:T(8,128)(2,1)} %get-tuple-element.225, s32[]{:T(128)S(6)} %select_n.67, s32[]{:T(128)S(6)} %select_n.69, s32[]{:T(128)S(6)} %select_n.68), kind=kOutput, calls=%fused_computation.40.clone.1 | convolution fusion | flops 404225024 | bytes 1583104 | tf_op jit(solution)/shard_map/while/body/eval_jaxpr/dot_general | solution.py:43
  175.7 0.2 dynamic_update_slice.23
  176.0 0.6 fusion.26
  179.7 2.2 %fusion.28 = (f32[512]{0:T(512)S(1)}, f32[512]{0:T(512)S(1)}) fusion(f32[512]{0:T(512)S(1)} %bitcast.71, f32[512]{0:T(512)S(1)} %bitcast.70, bf16[2,2048,768]{2,1,0:T(8,128)(2,1)} %get-tuple-element.225, s32[]{:T(128)S(6)} %select_n.67, s32[]{:T(128)S(6)} %select_n.69, s32[]{:T(128)S(6)} %select_n.68), kind=kOutput, calls=%fused_computation.40.clone.1 | convolution fusion | flops 404225024 | bytes 1583104 | tf_op jit(solution)/shard_map/while/body/eval_jaxpr/dot_general | solution.py:43
  182.0 0.2 dynamic_update_slice.22
  182.6 0.6 fusion.26
  186.4 2.2 %fusion.28 = (f32[512]{0:T(512)S(1)}, f32[512]{0:T(512)S(1)}) fusion(f32[512]{0:T(512)S(1)} %bitcast.71, f32[512]{0:T(512)S(1)} %bitcast.70, bf16[2,2048,768]{2,1,0:T(8,128)(2,1)} %get-tuple-element.225, s32[]{:T(128)S(6)} %select_n.67, s32[]{:T(128)S(6)} %select_n.69, s32[]{:T(128)S(6)} %select_n.68), kind=kOutput, calls=%fused_computation.40.clone.1 | convolution fusion | flops 404225024 | bytes 1583104 | tf_op jit(solution)/shard_map/while/body/eval_jaxpr/dot_general | solution.py:43
  189.1 3.5 %all-reduce = f32[2,2,1024]{2,0,1:T(2,128)S(1)} all-reduce(f32[2,2,1024]{2,0,1:T(2,128)S(1)} %bitcast.69), channel_id=2, replica_groups=mesh['groups'=2,'owner'=8,'tile'=2] {'tile'}, use_global_device_ids=true, to_apply=%region_10.11.clone | all-reduce | flops 4096 | bytes 32768
  192.6 0.6 dynamic-slice_bitcast_fusion
  193.2 8.9 %all_to_all.16 = f32[2,8,128]{2,0,1:T(2,128)S(1)} all-to-all(f32[2,8,128]{2,0,1:T(2,128)S(1)} %dynamic-slice_bitcast_fusion), channel_id=1, replica_groups=mesh['groups'=2,'owner'=8,'tile'=2] {'owner'}, dimensions={1} | all-to-all | bytes 16384 | tf_op jit(solution)/shard_map/all_to_all | solution.py:110
  202.1 6.1 %gather_fusion = f32[1024]{0:T(1024)S(1)} fusion(f32[2048]{0:T(1024)S(1)} %bitcast.65, s32[1024]{0:T(1024)S(1)} %get-tuple-element.150), kind=kCustom, calls=%fused_computation | custom fusion | bytes 12288 | tf_op jit(solution)/shard_map/gather | solution.py:113
  208.2 0.6 log.3
  (82 shorter events, 6.2 us)
Async XLA Ops:
  6.5 116.1 %all-gather.2.cloned.1.call-start = ((), (), s32[]{:S(2)}) async-start(), calls=%async_computation.3 | async-start | bytes 9437184 | tf_op jit(solution)/shard_map/all_gather | solution.py:99
  102.6 11.8 %copy-start = (s32[10,2,3]{0,2,1:T(4,128)S(1)}, s32[10,2,3]{0,2,1:T(4,128)}, u32[]{:S(2)}) copy-start(s32[10,2,3]{0,2,1:T(4,128)} %constant.123.clone) | copy-start | bytes 724
  102.6 11.8 %copy-start.1 = (u32[32]{0:T(128)S(1)}, u32[32]{0:T(128)}, u32[]{:S(2)}) copy-start(u32[32]{0:T(128)} %constant.126) | copy-start | bytes 388
  110.8 10.0 %all-to-all-start.1 = ((bf16[2,8,128]{2,0,1:T(2,128)(2,1)}), bf16[2,8,128]{2,0,1:T(2,128)(2,1)S(1)}, u32[]{:S(2)}, u32[]{:S(2)}) async-start(bf16[2,8,128]{2,0,1:T(2,128)(2,1)} %copy.23), calls=%async_computation.1 | async-start | bytes 8192 | tf_op jit(solution)/shard_map/all_to_all | solution.py:90
Sparse Core Ops, SparseCore 0:
  102.7 15.7 all-gather.1
where the time goes:
time: 217 us; the launch traced here: 216 us
  blocking collectives  91.9 us (42%)
  loops' own time  31.9 us (15%)
  local copies, waits for them, and re-layouts  29.8 us (14%)
  matrix products  21.9 us (10%)
  other arithmetic  17.4 us (8%)
  between operations  13.5 us (6%)
  waiting for transfers between devices  5.76 us (3%)
  starting transfers between devices  3.59 us (2%)
    all_to_all x1, blocking collectives, shards(): lax.all_to_all(outgoing.reshape(CLUS_OWN, owners, capacity, width), 'owne...  77.8 us
    another operation x1, loops' own time, kernel_sums(): return lax.fori_loop(0, table.shape[0], one_pair, start)  31.9 us
    dot_general x10, matrix products, one_pair(): lax.dot_general(left, right, (((1,), (1,)), ((), ())), preferred_element_...  21.9 us
    all_to_all x1, blocking collectives, shards(): lax.all_to_all(shares.reshape(CLUS_OWN, owners, capacity), 'owner', split...  8.88 us
    scatter x1, local copies, waits for them, and re-layouts, shards(): flags = jnp.zeros((clusters * capacity,), jnp.bfloat16).at[target].set(jn...  7.59 us
    scatter x1, other arithmetic, shards(): jnp.zeros((clusters * capacity, width), jnp.bfloat16).at[target].set(unit)  7.17 us
    gather x1, local copies, waits for them, and re-layouts, shards(): score = returned.reshape(-1)[target]  6.15 us
    all_to_all x1, waiting for transfers between devices, shards(): lax.all_to_all(flags.reshape(CLUS_OWN, owners, capacity), 'owner', split_...  5.72 us
  transfers between devices with their start and end apart: 2, of which 1 were waited for; matrix products, arithmetic and copies ran while one was open for 4% of the time, Pallas kernels for 0%

commit v1 on v0

v1 whole, which is shorter than its diff:
```python
import functools

import jax
import jax.numpy as jnp
from jax import lax
from jax.experimental import pallas as pl
from jax.experimental.pallas import tpu as pltpu
from jax.sharding import PartitionSpec as P

CLUS_OWN = 2
LANES = 128
MESH = pl.DeviceIdType.MESH

epsilon = 1e-06
sharpness = 20.0


def flipped(index, offset, count):
    total = 0
    bit = 1
    while bit < count:
        digit = lax.rem(lax.div(index, bit) + lax.div(offset, bit), 2)
        total = total + digit * bit
        bit *= 2
    return total


def fold(values):
    rows, lanes = values.shape
    return jnp.sum(values.reshape(rows // 8, 8, lanes), axis=0)


def dup_kernel(
    n, cap, x_ref, id_ref, out_ref,
    unit, within_ref, chosen, outgoing, held, count_out, count_in, sums,
    score_out, score_in, spread,
    send_sem, recv_sem, csend_sem, crecv_sem,
    fsend_sem, frecv_sem, fcsend_sem, fcrecv_sem, rsend_sem, rrecv_sem,
):
    rows, width = x_ref.shape
    clusters = CLUS_OWN * n
    me = lax.axis_index("owner").astype(jnp.int32)
    other = 1 - lax.axis_index("tile").astype(jnp.int32)

    barrier = pltpu.get_barrier_semaphore()

    def greet(q, carry):
        pl.semaphore_signal(
            barrier, inc=1, device_id={"owner": flipped(me, q, n)}, device_id_type=MESH
        )
        return carry

    lax.fori_loop(1, n, greet, 0)
    pl.semaphore_signal(barrier, inc=1, device_id={"tile": other}, device_id_type=MESH)

    def rows_copy(q):
        return pltpu.make_async_remote_copy(
            src_ref=outgoing.at[q], dst_ref=held.at[0, q],
            send_sem=send_sem.at[q], recv_sem=recv_sem.at[q],
            device_id={"owner": flipped(me, q, n)}, device_id_type=MESH,
        )

    def count_copy(q):
        return pltpu.make_async_remote_copy(
            src_ref=count_out.at[q], dst_ref=count_in.at[0, q],
            send_sem=csend_sem.at[q], recv_sem=crecv_sem.at[q],
            device_id={"owner": flipped(me, q, n)}, device_id_type=MESH,
        )

    def rows_forward(q):
        return pltpu.make_async_remote_copy(
            src_ref=held.at[0, q], dst_ref=held.at[1, q],
            send_sem=fsend_sem.at[q], recv_sem=frecv_sem.at[q],
            device_id={"tile": other}, device_id_type=MESH,
        )

    def count_forward(q):
        return pltpu.make_async_remote_copy(
            src_ref=count_in.at[0, q], dst_ref=count_in.at[1, q],
            send_sem=fcsend_sem.at[q], recv_sem=fcrecv_sem.at[q],
            device_id={"tile": other}, device_id_type=MESH,
        )

    def score_copy(q):
        return pltpu.make_async_remote_copy(
            src_ref=score_out.at[q], dst_ref=score_in.at[q],
            send_sem=rsend_sem.at[q], recv_sem=rrecv_sem.at[q],
            device_id={"owner": flipped(me, q, n)}, device_id_type=MESH,
        )

    piece = 128

    def normalise(step, carry):
        at = pl.ds(pl.multiple_of(step * piece, piece), piece)
        values = x_ref[at, :].astype(jnp.float32)
        scale = lax.rsqrt(jnp.sum(values * values, axis=1, keepdims=True) + epsilon)
        unit[at, :] = (values * scale).astype(jnp.bfloat16)
        return carry

    lax.fori_loop(0, rows // piece, normalise, 0)

    ids = id_ref[...]
    member = lax.broadcasted_iota(jnp.int32, (clusters, rows), 0) == ids
    onehot = jnp.where(member, 1.0, 0.0)
    ranks = jnp.zeros((clusters, rows), jnp.float32)
    for first in range(0, rows, piece):
        earlier = (
            lax.broadcasted_iota(jnp.int32, (piece, rows), 0) + first
            < lax.broadcasted_iota(jnp.int32, (piece, rows), 1)
        )
        ranks += jnp.dot(
            onehot[:, first : first + piece].astype(jnp.bfloat16),
            jnp.where(earlier, 1.0, 0.0).astype(jnp.bfloat16),
            preferred_element_type=jnp.float32,
        )
    within_ref[...] = jnp.sum(onehot * ranks, axis=0, keepdims=True)

    def pack(q, rows_ref, counts_ref):
        target = CLUS_OWN * flipped(me, q, n)
        within = within_ref[...]
        slots = lax.broadcasted_iota(jnp.int32, (cap, rows), 0).astype(jnp.float32)
        picks = []
        for c in range(CLUS_OWN):
            here = id_ref[...] == target + c
            key = jnp.where(here, within, -1.0)
            picks.append(jnp.where(slots == key, 1.0, 0.0).astype(jnp.bfloat16))
            count = jnp.sum(jnp.where(here, 1.0, 0.0), axis=1, keepdims=True)
            counts_ref[c : c + 1, :] = jnp.broadcast_to(count, (1, LANES))
        pick = jnp.concatenate(picks, axis=0)
        rows_ref[...] = jnp.dot(
            pick, unit[...], preferred_element_type=jnp.float32
        ).astype(jnp.bfloat16)

    def clear(q, carry):
        count_out[q] = jnp.zeros((8, LANES), jnp.float32)
        score_out[q] = jnp.zeros((8, LANES), jnp.float32)
        for c in range(CLUS_OWN):
            sums[q, c] = jnp.zeros((8, cap), jnp.float32)
        return carry

    lax.fori_loop(0, n, clear, 0)
    score_in[0] = jnp.zeros((8, LANES), jnp.float32)
    count_in[0, 0] = jnp.zeros((8, LANES), jnp.float32)
    pl.semaphore_wait(barrier, n)

    def send(q, carry):
        pack(q, outgoing.at[q], count_out.at[q])
        rows_copy(q).start()
        count_copy(q).start()
        return carry

    lax.fori_loop(n // 2, n, send, 0)
    lax.fori_loop(1, n // 2, send, 0)
    pack(0, held.at[0, 0], count_in.at[0, 0])

    def block(u, a, c):
        return held[u, a, c * cap : (c + 1) * cap, :]

    def add_pair(u, b, a, c):
        cosine = lax.dot_general(
            block(u, b, c), block(0, a, c), (((1,), (1,)), ((), ())),
            preferred_element_type=jnp.float32,
        )
        live = lax.broadcasted_iota(jnp.int32, (cap, cap), 0).astype(jnp.float32) < (
            count_in[u, b, c : c + 1, 0:cap]
        )
        shift = jnp.where(live, -sharpness, -1e30)
        return fold(jnp.exp(cosine * sharpness + shift))

    def work(k):
        rows_forward(k).start()
        count_forward(k).start()

        def early(a, carry):
            new = []
            for c in range(CLUS_OWN):
                sums[a, c] += add_pair(0, k, a, c)
                new.append(carry[c] + add_pair(0, a, k, c) + add_pair(1, a, k, c))
            return tuple(new)

        mine = lax.fori_loop(
            0, k, early, tuple(jnp.zeros((8, cap), jnp.float32) for _ in range(CLUS_OWN))
        )
        for c in range(CLUS_OWN):
            sums[k, c] += mine[c] + add_pair(0, k, k, c)
        rows_forward(k).wait_recv()
        count_forward(k).wait_recv()

        def late(a, carry):
            for c in range(CLUS_OWN):
                sums[a, c] += add_pair(1, k, a, c)
            return carry

        lax.fori_loop(0, k + 1, late, 0)

    work(0)
    spread[...] = jnp.where(
        lax.broadcasted_iota(jnp.int32, (LANES, rows), 0).astype(jnp.float32) == within_ref[...],
        1.0, 0.0,
    )

    def arrive(k, carry):
        rows_copy(k).wait_recv()
        count_copy(k).wait_recv()
        work(k)
        return carry

    lax.fori_loop(1, n, arrive, 0)

    def give_back(q, carry):
        for c in range(CLUS_OWN):
            score_out[q, c : c + 1, 0:cap] = jnp.sum(sums[q, c], axis=0, keepdims=True)
        score_copy(q).start()
        return carry

    lax.fori_loop(1, n, give_back, 0)
    for c in range(CLUS_OWN):
        score_in[0, c : c + 1, 0:cap] = jnp.sum(sums[0, c], axis=0, keepdims=True)

    def finish(q, carry):
        rows_copy(q).wait_send()
        count_copy(q).wait_send()
        return carry

    lax.fori_loop(1, n, finish, 0)

    def finish_forward(q, carry):
        rows_forward(q).wait_send()
        count_forward(q).wait_send()
        return carry

    lax.fori_loop(0, n, finish_forward, 0)

    def collect(q, carry):
        score_copy(q).wait()
        return carry

    lax.fori_loop(1, n, collect, 0)

    chosen[...] = jnp.dot(
        score_in[...].reshape(n * 8, LANES), spread[...],
        preferred_element_type=jnp.float32, precision=lax.Precision.HIGHEST,
    ).reshape(n, 8, rows)

    def choose(q, total):
        target = CLUS_OWN * flipped(me, q, n)
        for c in range(CLUS_OWN):
            total = total + jnp.where(id_ref[...] == target + c, chosen[q, c : c + 1, :], 0.0)
        return total

    score = lax.fori_loop(0, n, choose, jnp.zeros((1, rows), jnp.float32))
    out_ref[...] = jnp.log(score)


def shards(embeddings, cluster_ids):
    n = lax.axis_size("owner")
    rows, width = embeddings.shape
    cap = 2 * rows // (CLUS_OWN * n)
    dma = pltpu.SemaphoreType.DMA
    result = pl.pallas_call(
        functools.partial(dup_kernel, n, cap),
        out_shape=jax.ShapeDtypeStruct((1, rows), jnp.float32),
        in_specs=[pl.BlockSpec(memory_space=pltpu.VMEM)] * 2,
        out_specs=pl.BlockSpec(memory_space=pltpu.VMEM),
        scratch_shapes=[
            pltpu.VMEM((rows, width), jnp.bfloat16),
            pltpu.VMEM((1, rows), jnp.float32),
            pltpu.VMEM((n, 8, rows), jnp.float32),
            pltpu.VMEM((n, CLUS_OWN * cap, width), jnp.bfloat16),
            pltpu.VMEM((2, n, CLUS_OWN * cap, width), jnp.bfloat16),
            pltpu.VMEM((n, 8, LANES), jnp.float32),
            pltpu.VMEM((2, n, 8, LANES), jnp.float32),
            pltpu.VMEM((n, CLUS_OWN, 8, cap), jnp.float32),
            pltpu.VMEM((n, 8, LANES), jnp.float32),
            pltpu.VMEM((n, 8, LANES), jnp.float32),
            pltpu.VMEM((LANES, rows), jnp.float32),
        ] + [dma((n,))] * 10,
        compiler_params=pltpu.CompilerParams(
            collective_id=0, has_side_effects=True, vmem_limit_bytes=48 * 1024 * 1024
        ),
    )(embeddings, cluster_ids.reshape(1, rows))
    return result.reshape(rows)


def solution(mesh):
    placed = (P(("groups", "owner", "tile"), None), P(("groups", "owner", "tile")))
    return jax.shard_map(
        shards,
        mesh=mesh,
        in_specs=placed,
        out_specs=P(("groups", "owner", "tile")),
        check_vma=False,
    )
```

time: 217 us -> 90.8 us (0.42)
  blocking collectives: 91.9 us -> 0 us
  Pallas kernels: 0 us -> 88 us
  loops' own time: 31.9 us -> 0 us
  local copies, waits for them, and re-layouts: 29.8 us -> 2.69 us
  matrix products: 21.9 us -> 0 us
  other arithmetic: 17.4 us -> 0 us
  between operations: 13.5 us -> 0.01 us
  waiting for transfers between devices: 5.76 us -> 0 us
  starting transfers between devices: 3.59 us -> 0 us
    pallas_call x0 -> x1, Pallas kernels: none -> 88 us  [shards(): pl.pallas_call(functools.partial(dup_kernel, n, cap), out_shape=jax.Shape...]
    all_to_all x2 -> x0, blocking collectives: 86.7 us -> none  [the longest x1 77.8 us: shards(): lax.all_to_all(outgoing.reshape(CLUS_OWN, owners, capacity, width), 'owne...]
    another operation x1 -> x0, loops' own time: 31.9 us -> none  [kernel_sums(): return lax.fori_loop(0, table.shape[0], one_pair, start)]
    dot_general x10 -> x0, matrix products: 21.9 us -> none  [one_pair(): lax.dot_general(left, right, (((1,), (1,)), ((), ())), preferred_element_...]
    scatter x1 -> x0, local copies, waits for them, and re-layouts: 7.59 us -> none  [shards(): flags = jnp.zeros((clusters * capacity,), jnp.bfloat16).at[target].set(jn...]
    scatter x1 -> x0, other arithmetic: 7.17 us -> none  [shards(): jnp.zeros((clusters * capacity, width), jnp.bfloat16).at[target].set(unit)]
    gather x1 -> x0, local copies, waits for them, and re-layouts: 6.15 us -> none  [shards(): score = returned.reshape(-1)[target]]
    all_to_all x1 -> x0, waiting for transfers between devices: 5.72 us -> none  [shards(): lax.all_to_all(flags.reshape(CLUS_OWN, owners, capacity), 'owner', split_...]
  transfers between devices with their start and end apart: 2 -> 0, of which waited for: 1 -> 0; matrix products, arithmetic and copies ran while one was open for 4% -> 0% of each run, Pallas kernels for 0% -> 0%
where the time goes in v1:
time: 90.8 us; the launch traced here: 90.7 us
  Pallas kernels  88 us (97%)
  local copies, waits for them, and re-layouts  2.69 us (3%)
    pallas_call x1, Pallas kernels, shards(): pl.pallas_call(functools.partial(dup_kernel, n, cap), out_shape=jax.Shape...  88 us
    unnamed x5, local copies, waits for them, and re-layouts  2.69 us

profile of v1, /device:TPU:0, one launch (start us, length us, event | category | flops | bytes accessed | tf_op | source)
XLA Modules:
  0.0 90.7 jit_solution(18152391220505602562)
XLA Ops:
  0.0 0.0 copy-start
  0.0 1.4 %copy-done = bf16[1024,768]{1,0:T(8,128)(2,1)S(1)} copy-done((bf16[1024,768]{1,0:T(8,128)(2,1)S(1)}, bf16[1024,768]{1,0:T(8,128)(2,1)}, u32[]{:S(2)}) %copy-start) | copy-done | bytes 1572888
  1.4 0.0 copy-start.1
  1.4 0.7 copy-done.1
  2.1 88.0 %shard_map.28 = f32[1,1024]{1,0:T(1,128)S(1)} custom-call(bf16[1024,768]{1,0:T(8,128)(2,1)S(1)} %copy-done, s32[1,1024]{1,0:T(1,128)S(1)} %bitcast.3), custom_call_target="tpu_custom_call" | custom-call | tf_op jit(solution)/shard_map/pallas_call | solution.py:260
  90.1 0.6 copy.4
Async XLA Ops:
  0.0 1.4 %copy-start = (bf16[1024,768]{1,0:T(8,128)(2,1)S(1)}, bf16[1024,768]{1,0:T(8,128)(2,1)}, u32[]{:S(2)}) copy-start(bf16[1024,768]{1,0:T(8,128)(2,1)} %x_ref.1) | copy-start | bytes 4718596
  1.4 0.7 copy-start.1

commit v2 on v1

--- a/solution.py
+++ b/solution.py
@@ -31,13 +31,17 @@
 
 
 def dup_kernel(
-    n, cap, x_ref, id_ref, out_ref,
-    unit, within_ref, chosen, outgoing, held, count_out, count_in, sums,
+    n, cap, x_hbm, id_hbm, out_ref,
+    x_ref, id_ref, load_sem, unit, within_ref, chosen, outgoing, held, count_out, count_in, sums,
     score_out, score_in, spread,
     send_sem, recv_sem, csend_sem, crecv_sem,
     fsend_sem, frecv_sem, fcsend_sem, fcrecv_sem, rsend_sem, rrecv_sem,
 ):
     rows, width = x_ref.shape
+    load_ids = pltpu.make_async_copy(id_hbm, id_ref, load_sem.at[0])
+    load_rows = pltpu.make_async_copy(x_hbm, x_ref, load_sem.at[1])
+    load_ids.start()
+    load_rows.start()
     clusters = CLUS_OWN * n
     me = lax.axis_index("owner").astype(jnp.int32)
     other = 1 - lax.axis_index("tile").astype(jnp.int32)
@@ -88,7 +92,23 @@
             device_id={"owner": flipped(me, q, n)}, device_id_type=MESH,
         )
 
+    load_ids.wait()
+    ids = id_ref[...]
+    member = lax.broadcasted_iota(jnp.int32, (clusters, rows), 0) == ids
+    onehot = jnp.where(member, 1.0, 0.0)
     piece = 128
+    ranks = jnp.zeros((clusters, rows), jnp.float32)
+    for first in range(0, rows, piece):
+        earlier = (
+            lax.broadcasted_iota(jnp.int32, (piece, rows), 0) + first
+            < lax.broadcasted_iota(jnp.int32, (piece, rows), 1)
+        )
+        ranks += jnp.dot(
+            onehot[:, first : first + piece].astype(jnp.bfloat16),
+            jnp.where(earlier, 1.0, 0.0).astype(jnp.bfloat16),
+            preferred_element_type=jnp.float32,
+        )
+    within_ref[...] = jnp.sum(onehot * ranks, axis=0, keepdims=True)
 
     def normalise(step, carry):
         at = pl.ds(pl.multiple_of(step * piece, piece), piece)
@@ -97,23 +117,8 @@
         unit[at, :] = (values * scale).astype(jnp.bfloat16)
         return carry
 
+    load_rows.wait()
     lax.fori_loop(0, rows // piece, normalise, 0)
-
-    ids = id_ref[...]
-    member = lax.broadcasted_iota(jnp.int32, (clusters, rows), 0) == ids
-    onehot = jnp.where(member, 1.0, 0.0)
-    ranks = jnp.zeros((clusters, rows), jnp.float32)
-    for first in range(0, rows, piece):
-        earlier = (
-            lax.broadcasted_iota(jnp.int32, (piece, rows), 0) + first
-            < lax.broadcasted_iota(jnp.int32, (piece, rows), 1)
-        )
-        ranks += jnp.dot(
-            onehot[:, first : first + piece].astype(jnp.bfloat16),
-            jnp.where(earlier, 1.0, 0.0).astype(jnp.bfloat16),
-            preferred_element_type=jnp.float32,
-        )
-    within_ref[...] = jnp.sum(onehot * ranks, axis=0, keepdims=True)
 
     def pack(q, rows_ref, counts_ref):
         target = CLUS_OWN * flipped(me, q, n)
@@ -141,6 +146,7 @@
     lax.fori_loop(0, n, clear, 0)
     score_in[0] = jnp.zeros((8, LANES), jnp.float32)
     count_in[0, 0] = jnp.zeros((8, LANES), jnp.float32)
+    pack(n // 2, outgoing.at[n // 2], count_out.at[n // 2])
     pl.semaphore_wait(barrier, n)
 
     def send(q, carry):
@@ -149,23 +155,37 @@
         count_copy(q).start()
         return carry
 
-    lax.fori_loop(n // 2, n, send, 0)
+    def paced(q, carry):
+        pack(q, outgoing.at[q], count_out.at[q])
+        rows_copy(q - 2).wait_send()
+        rows_copy(q).start()
+        count_copy(q).start()
+        return carry
+    rows_copy(n // 2).start()
+    count_copy(n // 2).start()
+    lax.fori_loop(n // 2 + 1, n // 2 + 2, send, 0)
     lax.fori_loop(1, n // 2, send, 0)
+    lax.fori_loop(n // 2 + 2, n, paced, 0)
     pack(0, held.at[0, 0], count_in.at[0, 0])
+
+    def both(a, c):
+        return jnp.concatenate([block(0, a, c), block(1, a, c)], axis=0)
 
     def block(u, a, c):
         return held[u, a, c * cap : (c + 1) * cap, :]
 
-    def add_pair(u, b, a, c):
+    def add_pair(b, a, c):
         cosine = lax.dot_general(
-            block(u, b, c), block(0, a, c), (((1,), (1,)), ((), ())),
+            both(b, c), block(0, a, c), (((1,), (1,)), ((), ())),
             preferred_element_type=jnp.float32,
         )
-        live = lax.broadcasted_iota(jnp.int32, (cap, cap), 0).astype(jnp.float32) < (
-            count_in[u, b, c : c + 1, 0:cap]
-        )
-        shift = jnp.where(live, -sharpness, -1e30)
-        return fold(jnp.exp(cosine * sharpness + shift))
+        slot = lax.broadcasted_iota(jnp.int32, (cap, cap), 0).astype(jnp.float32)
+        total = jnp.zeros((8, cap), jnp.float32)
+        for u in range(2):
+            live = slot < count_in[u, b, c : c + 1, 0:cap]
+            shift = jnp.where(live, -sharpness, -1e30)
+            total += fold(jnp.exp(cosine[u * cap : (u + 1) * cap] * sharpness + shift))
+        return total
 
     def work(k):
         rows_forward(k).start()
@@ -174,24 +194,62 @@
         def early(a, carry):
             new = []
             for c in range(CLUS_OWN):
-                sums[a, c] += add_pair(0, k, a, c)
-                new.append(carry[c] + add_pair(0, a, k, c) + add_pair(1, a, k, c))
+                new.append(carry[c] + add_pair(a, k, c))
             return tuple(new)
 
         mine = lax.fori_loop(
             0, k, early, tuple(jnp.zeros((8, cap), jnp.float32) for _ in range(CLUS_OWN))
         )
         for c in range(CLUS_OWN):
-            sums[k, c] += mine[c] + add_pair(0, k, k, c)
+            sums[k, c] = mine[c]
         rows_forward(k).wait_recv()
         count_forward(k).wait_recv()
 
         def late(a, carry):
             for c in range(CLUS_OWN):
-                sums[a, c] += add_pair(1, k, a, c)
+                sums[a, c] += add_pair(k, a, c)
             return carry
 
         lax.fori_loop(0, k + 1, late, 0)
+
+    def wide(first, last, c):
+        at = slice(c * cap, (c + 1) * cap)
+        return held[0, first:last, at, :].reshape((last - first) * cap, width)
+
+    def kernels(left, right, lives):
+        cosine = lax.dot_general(
+            left, right, (((1,), (1,)), ((), ())), preferred_element_type=jnp.float32
+        )
+        lanes = right.shape[0]
+        slot = lax.broadcasted_iota(jnp.int32, (cap, cap), 0).astype(jnp.float32)
+        parts = []
+        shifts = [jnp.where(slot < live[:, 0:cap], -sharpness, -1e30) for live in lives]
+        for lane in range(0, lanes, cap):
+            total = jnp.zeros((8, cap), jnp.float32)
+            for b, shift in enumerate(shifts):
+                piece_cos = cosine[b * cap : (b + 1) * cap, lane : lane + cap]
+                total += fold(jnp.exp(piece_cos * sharpness + shift))
+            parts.append(total)
+        return parts
+
+    def work_fixed(k):
+        rows_forward(k).start()
+        count_forward(k).start()
+        for c in range(CLUS_OWN):
+            total = jnp.zeros((8, cap), jnp.float32)
+            for b in range(k):
+                lives = [count_in[u, b, c : c + 1, :] for u in range(2)]
+                total += kernels(both(b, c), block(0, k, c), lives)[0]
+            sums[k, c] = total
+        rows_forward(k).wait_recv()
+        count_forward(k).wait_recv()
+        for c in range(CLUS_OWN):
+            lives = [count_in[u, k, c : c + 1, :] for u in range(2)]
+            for a in range(0, k + 1, 2):
+                last = min(a + 2, k + 1)
+                parts = kernels(both(k, c), wide(a, last, c), lives)
+                for i in range(last - a):
+                    sums[a + i, c] += parts[i]
 
     work(0)
     spread[...] = jnp.where(
@@ -205,7 +263,13 @@
         work(k)
         return carry
 
-    lax.fori_loop(1, n, arrive, 0)
+    if n <= 8:
+        for k in range(1, n):
+            rows_copy(k).wait_recv()
+            count_copy(k).wait_recv()
+            work_fixed(k)
+    else:
+        lax.fori_loop(1, n, arrive, 0)
 
     def give_back(q, carry):
         for c in range(CLUS_OWN):
@@ -218,10 +282,15 @@
         score_in[0, c : c + 1, 0:cap] = jnp.sum(sums[0, c], axis=0, keepdims=True)
 
     def finish(q, carry):
+        count_copy(q).wait_send()
+        return carry
+
+    def finish_rows(q, carry):
         rows_copy(q).wait_send()
-        count_copy(q).wait_send()
-        return carry
-
+        return carry
+
+    lax.fori_loop(1, n // 2, finish_rows, 0)
+    lax.fori_loop(n - 2, n, finish_rows, 0)
     lax.fori_loop(1, n, finish, 0)
 
     def finish_forward(q, carry):
@@ -260,9 +329,12 @@
     result = pl.pallas_call(
         functools.partial(dup_kernel, n, cap),
         out_shape=jax.ShapeDtypeStruct((1, rows), jnp.float32),
-        in_specs=[pl.BlockSpec(memory_space=pltpu.VMEM)] * 2,
+        in_specs=[pl.BlockSpec(memory_space=pl.ANY)] * 2,
         out_specs=pl.BlockSpec(memory_space=pltpu.VMEM),
         scratch_shapes=[
+            pltpu.VMEM((rows, width), jnp.bfloat16),
+            pltpu.VMEM((1, rows), jnp.int32),
+            dma((2,)),
             pltpu.VMEM((rows, width), jnp.bfloat16),
             pltpu.VMEM((1, rows), jnp.float32),
             pltpu.VMEM((n, 8, rows), jnp.float32),

time: 90.8 us -> 86.6 us (0.954)
  Pallas kernels: 88 us -> 83.7 us
    pallas_call x1, Pallas kernels: 88 us -> 83.7 us  [shards(): pl.pallas_call(functools.partial(dup_kernel, n, cap), out_shape=jax.Shape...]
where the time goes in v2:
time: 86.6 us; the launch traced here: 86.4 us
  Pallas kernels  83.7 us (97%)
  local copies, waits for them, and re-layouts  2.69 us (3%)
    pallas_call x1, Pallas kernels, shards(): pl.pallas_call(functools.partial(dup_kernel, n, cap), out_shape=jax.Shape...  83.7 us
    unnamed x5, local copies, waits for them, and re-layouts  2.69 us

profile of v2, /device:TPU:0, one launch (start us, length us, event | category | flops | bytes accessed | tf_op | source)
XLA Modules:
  0.0 86.4 jit_solution(2065430918600444818)
XLA Ops:
  0.0 0.0 copy-start
  0.0 1.4 %copy-done = bf16[1024,768]{1,0:T(8,128)(2,1)S(1)} copy-done((bf16[1024,768]{1,0:T(8,128)(2,1)S(1)}, bf16[1024,768]{1,0:T(8,128)(2,1)}, u32[]{:S(2)}) %copy-start) | copy-done | bytes 1572888
  1.4 0.0 copy-start.1
  1.4 0.7 copy-done.1
  2.1 83.7 %shard_map.28 = f32[1,1024]{1,0:T(1,128)S(1)} custom-call(bf16[1024,768]{1,0:T(8,128)(2,1)S(1)} %copy-done, s32[1,1024]{1,0:T(1,128)S(1)} %bitcast.3), custom_call_target="tpu_custom_call" | custom-call | tf_op jit(solution)/shard_map/pallas_call | solution.py:329
  85.8 0.6 copy.4
Async XLA Ops:
  0.0 1.4 %copy-start = (bf16[1024,768]{1,0:T(8,128)(2,1)S(1)}, bf16[1024,768]{1,0:T(8,128)(2,1)}, u32[]{:S(2)}) copy-start(bf16[1024,768]{1,0:T(8,128)(2,1)} %x_hbm.1) | copy-start | bytes 4718596
  1.4 0.7 copy-start.1

commit v3 on v2

--- a/solution.py
+++ b/solution.py
@@ -16,6 +16,8 @@
 
 
 def flipped(index, offset, count):
+    far = count // 2
+    offset = jnp.where(offset < far, offset, offset + 1 - 2 * lax.rem(offset, 2))
     total = 0
     bit = 1
     while bit < count:
@@ -318,7 +320,7 @@
         return total
 
     score = lax.fori_loop(0, n, choose, jnp.zeros((1, rows), jnp.float32))
-    out_ref[...] = jnp.log(score)
+    out_ref[...] = score
 
 
 def shards(embeddings, cluster_ids):
@@ -351,7 +353,7 @@
             collective_id=0, has_side_effects=True, vmem_limit_bytes=48 * 1024 * 1024
         ),
     )(embeddings, cluster_ids.reshape(1, rows))
-    return result.reshape(rows)
+    return jnp.log(result.reshape(rows))
 
 
 def solution(mesh):

time: 86.6 us -> 85.7 us (0.990)
    unnamed x5 -> x4, local copies, waits for them, and re-layouts: 2.69 us -> 2.09 us
where the time goes in v3:
time: 85.7 us; the launch traced here: 85.6 us
  Pallas kernels  82.9 us (97%)
  local copies, waits for them, and re-layouts  2.7 us (3%)
    pallas_call x1, Pallas kernels, shards(): pl.pallas_call(functools.partial(dup_kernel, n, cap), out_shape=jax.Shape...  82.9 us
    unnamed x4, local copies, waits for them, and re-layouts  2.09 us

profile of v3, /device:TPU:0, one launch (start us, length us, event | category | flops | bytes accessed | tf_op | source)
XLA Modules:
  0.0 85.6 jit_solution(11810822836043805410)
XLA Ops:
  0.0 0.0 copy-start
  0.0 1.4 %copy-done = bf16[1024,768]{1,0:T(8,128)(2,1)S(1)} copy-done((bf16[1024,768]{1,0:T(8,128)(2,1)S(1)}, bf16[1024,768]{1,0:T(8,128)(2,1)}, u32[]{:S(2)}) %copy-start) | copy-done | bytes 1572888
  1.4 0.0 copy-start.1
  1.4 0.7 copy-done.1
  2.1 82.9 %shard_map.28 = f32[1,1024]{1,0:T(1,128)S(1)} custom-call(bf16[1024,768]{1,0:T(8,128)(2,1)S(1)} %copy-done, s32[1,1024]{1,0:T(1,128)S(1)} %bitcast.2), custom_call_target="tpu_custom_call" | custom-call | tf_op jit(solution)/shard_map/pallas_call | solution.py:331
  85.0 0.6 log.6
Async XLA Ops:
  0.0 1.4 %copy-start = (bf16[1024,768]{1,0:T(8,128)(2,1)S(1)}, bf16[1024,768]{1,0:T(8,128)(2,1)}, u32[]{:S(2)}) copy-start(bf16[1024,768]{1,0:T(8,128)(2,1)} %x_hbm.1) | copy-start | bytes 4718596
  1.4 0.7 copy-start.1
